TPU v7x, 32 devices: a whole 2x2x4 slice. The times are simulated.
32 devices in a mesh: wide: 8 (over z, core), narrow: 4 (over y, x).
Axes of the slice: x: 2, y: 2, z: 4, core: 2. Of those that a mesh axis runs over, the one named last changes fastest.
Arguments:
- block_states: bfloat16 [16, 64, 4096], P('wide', None, 'narrow'), may hold values from -6 to 6
- attn_gain: float32 [4096], replicated, may hold values from 0.1 to 1.9
- ffn_gain: float32 [4096], replicated, may hold values from 0.1 to 1.9
- final_gain: float32 [4096], replicated, may hold values from 0.1 to 1.9
- w_query: bfloat16 [4096, 4096], P(None, 'narrow'), may hold values from -0.09375 to 0.09375
- w_keyval: bfloat16 [4096, 1024], replicated, may hold values from -0.09375 to 0.09375
- w_out: bfloat16 [4096, 4096], P('narrow'), may hold values from -0.09375 to 0.09375
- w_gate: bfloat16 [4096, 1024], P(None, 'narrow'), may hold values from -0.09375 to 0.09375
- w_up: bfloat16 [4096, 1024], P(None, 'narrow'), may hold values from -0.09375 to 0.09375
- w_down: bfloat16 [1024, 4096], P('narrow'), may hold values from -0.1875 to 0.1875
- w_head: bfloat16 [4096, 32768], P(None, ('wide', 'narrow')), may hold values from -8 to 8
- cache: bfloat16 [16, 512, 4, 256], P('wide'), may hold values from -2000 to 2000
- prefix_lengths: int32 [16], P('wide'), may hold values from 128 to 512, as said below
- masked_positions: int32 [8, 64], replicated, may hold values from 0 to 63, as said below
Outputs:
- log_probs: float32 [512, 32768], P(None, ('wide', 'narrow'))
- confidence: float32 [8, 64], replicated
Inputs may be any that keep to these rules, and one draw needn't show every extreme that they name: `prefix_lengths`: some request branch has exactly 512 valid positions. `masked_positions`: the 64 positions of one request are distinct.
All inputs are finite; a program needn't handle non-finite values.
Results may differ from a plain program's by a relative error of at most 0.024.
The roundings to bfloat16 on the way count: a program that leaves them out, or rounds other values in their place, can miss the bound.
Values may be sent and summed in bfloat16 or wider, within the bound.
A program may use at most 128 MiB of HBM per device.

v0:
```python
import math

import jax
import jax.numpy as jnp
from jax import lax
from jax.sharding import PartitionSpec as P

D = 4096
KVH = 4
HD = 128


EPS = 1e-06
GUIDE = 1.5


def swapped(value, axis, bit):
    mask = 2**bit
    pairs = [(source, source ^ mask) for source in range(lax.axis_size(axis))]
    return lax.ppermute(value, axis, pairs)


def rms_scale(rows, gain):
    return rows * lax.rsqrt(jnp.mean(rows * rows, axis=-1, keepdims=True) + EPS) * gain


def split_halves(rows, is_upper, kept_count):
    lower_part = rows[:kept_count]
    upper_part = rows[kept_count:]
    outgoing = jnp.where(is_upper, lower_part, upper_part)
    own_rows = jnp.where(is_upper, upper_part, lower_part)
    return (outgoing, own_rows)


def guide_rows(own_rows, partner, is_upper):
    cond_rows = jnp.where(is_upper, partner, own_rows)
    uncond_rows = jnp.where(is_upper, own_rows, partner)
    return (uncond_rows + GUIDE * (cond_rows - uncond_rows)).astype(jnp.bfloat16)


def on_device(
    block_states,
    attn_gain,
    ffn_gain,
    final_gain,
    w_query,
    w_keyval,
    w_out,
    w_gate,
    w_up,
    w_down,
    w_head,
    cache,
    prefix_lengths,
    masked_positions,
):
    n_wide = lax.axis_size("wide")
    n_narrow = lax.axis_size("narrow")
    wide_index = lax.axis_index("wide")
    narrow_index = lax.axis_index("narrow")
    half_wide = n_wide // 2
    local_req = block_states.shape[0]
    kept_count = local_req // 2
    masked = masked_positions.shape[1]
    is_upper = wide_index >= half_wide
    share_cols = D // n_narrow
    full_rows = lax.all_gather(block_states, "narrow", axis=2, tiled=True)
    normed = rms_scale(full_rows.astype(jnp.float32), attn_gain).astype(jnp.bfloat16)
    kv_head = narrow_index // (n_narrow // KVH)
    head_weight = lax.dynamic_slice_in_dim(w_keyval, kv_head * (2 * HD), 2 * HD, 1)
    block_kv = jnp.einsum(
        "bld,dc->blc", normed, head_weight, preferred_element_type=jnp.float32
    ).astype(jnp.bfloat16)
    cache_kv = lax.dynamic_index_in_dim(cache, kv_head, axis=2, keepdims=False)
    first_req = wide_index % half_wide * local_req
    my_positions = lax.dynamic_slice_in_dim(masked_positions, first_req, local_req, 0)
    picked = jax.vmap(lambda rows, idx: rows[idx])(full_rows, my_positions)
    picked_normed = jax.vmap(lambda rows, idx: rows[idx])(normed, my_positions)
    local_heads = w_query.shape[1] // HD
    query = jnp.einsum(
        "bmd,dc->bmc", picked_normed, w_query, preferred_element_type=jnp.float32
    ).astype(jnp.bfloat16)
    query = query.reshape(local_req, masked, local_heads, HD)
    scale = 1.0 / math.sqrt(HD)
    pre_scores = (
        jnp.einsum("bmhd,bpd->bhmp", query, cache_kv[..., :HD], preferred_element_type=jnp.float32)
        * scale
    )
    live = jnp.arange(cache_kv.shape[1])[None, :] < prefix_lengths[:, None]
    pre_scores = jnp.where(live[:, None, None, :], pre_scores, -jnp.inf)
    blk_scores = (
        jnp.einsum("bmhd,bld->bhml", query, block_kv[..., :HD], preferred_element_type=jnp.float32)
        * scale
    )
    peak = jnp.maximum(
        jnp.max(pre_scores, axis=-1, keepdims=True), jnp.max(blk_scores, axis=-1, keepdims=True)
    )
    pre_weights = jnp.exp(pre_scores - peak)
    blk_weights = jnp.exp(blk_scores - peak)
    weight_total = jnp.sum(pre_weights, axis=-1, keepdims=True) + jnp.sum(
        blk_weights, axis=-1, keepdims=True
    )
    pre_probs = (pre_weights / weight_total).astype(jnp.bfloat16)
    blk_probs = (blk_weights / weight_total).astype(jnp.bfloat16)
    attended = jnp.einsum(
        "bhmp,bpd->bmhd", pre_probs, cache_kv[..., HD:], preferred_element_type=jnp.float32
    )
    attended = attended + jnp.einsum(
        "bhml,bld->bmhd", blk_probs, block_kv[..., HD:], preferred_element_type=jnp.float32
    )
    attended = attended.astype(jnp.bfloat16).reshape(local_req, masked, local_heads * HD)
    attn_part = jnp.einsum("bmc,cd->bmd", attended, w_out, preferred_element_type=jnp.float32)
    attn_total = lax.psum(attn_part, "narrow")
    first = picked.astype(jnp.float32) + attn_total
    ffn_in = rms_scale(first, ffn_gain).astype(jnp.bfloat16)
    first_share = lax.dynamic_slice_in_dim(first, narrow_index * share_cols, share_cols, 2)
    gate_act = jnp.einsum("bmd,dc->bmc", ffn_in, w_gate, preferred_element_type=jnp.float32)
    up_act = jnp.einsum("bmd,dc->bmc", ffn_in, w_up, preferred_element_type=jnp.float32)
    hidden = (jax.nn.silu(gate_act) * up_act).astype(jnp.bfloat16)
    ffn_part = jnp.einsum("bmc,cd->bmd", hidden, w_down, preferred_element_type=jnp.float32)
    swap_bit = n_wide.bit_length() - 2
    vocab_cols = w_head.shape[1]
    ffn_share = lax.psum_scatter(ffn_part, "narrow", scatter_dimension=2, tiled=True)
    second_share = first_share + ffn_share
    square_sum = lax.psum(jnp.sum(second_share * second_share, axis=-1), "narrow")
    gain_share = lax.dynamic_slice_in_dim(final_gain, narrow_index * share_cols, share_cols, 0)
    final = second_share * lax.rsqrt(square_sum / D + EPS)[..., None] * gain_share
    outgoing, own_rows = split_halves(final, is_upper, kept_count)
    partner = swapped(outgoing, "wide", swap_bit)
    guided = guide_rows(own_rows, partner, is_upper).reshape(kept_count * masked, share_cols)
    all_rows = lax.all_gather(guided, "wide", axis=0, tiled=True)
    logits = jnp.dot(
        lax.all_gather(all_rows, "narrow", axis=1, tiled=True),
        w_head,
        preferred_element_type=jnp.float32,
    )
    logits = logits.reshape(2, half_wide, kept_count, masked, vocab_cols)
    logits = jnp.transpose(logits, (1, 0, 2, 3, 4)).reshape(-1, vocab_cols)
    local_peak = jnp.max(logits, axis=-1)
    row_peak = lax.pmax(local_peak, ("wide", "narrow"))
    row_total = lax.psum(jnp.sum(jnp.exp(logits - row_peak[:, None]), axis=-1), ("wide", "narrow"))
    lse = row_peak + jnp.log(row_total)
    log_probs = logits - lse[:, None]
    confidence = jnp.exp(row_peak - lse).reshape(-1, masked)
    return (log_probs, confidence)


def solution(mesh):
    in_specs = (
        P("wide", None, "narrow"),
        P(),
        P(),
        P(),
        P(None, "narrow"),
        P(),
        P("narrow", None),
        P(None, "narrow"),
        P(None, "narrow"),
        P("narrow", None),
        P(None, ("wide", "narrow")),
        P("wide", None, None, None),
        P("wide"),
        P(),
    )
    out_specs = (P(None, ("wide", "narrow")), P())
    return jax.shard_map(
        on_device, mesh=mesh, in_specs=in_specs, out_specs=out_specs, check_vma=False
    )
```

profile of v0, /device:TPU:0, one launch (start us, length us, event | category | flops | bytes accessed | tf_op | source)
XLA Modules:
  0.0 377.7 jit_solution(13104650751558441493)
XLA Ops:
  8.0 0.7 fusion.59
  8.8 2.7 constant_dynamic-slice_fusion
  11.5 0.9 copy.68
  12.4 26.8 %all-gather.6.cloned.1.call-done = bf16[2,64,4096]{2,1,0:T(8,128)(2,1)} async-done(((bf16[2,64,1024]{2,1,0:T(8,128)(2,1)}), bf16[2,64,4096]{2,1,0:T(8,128)(2,1)}) %all-gather.6.cloned.1.call-update) | async-done | bytes 1048592 | tf_op jit(solution)/shard_map/all_gather | solution.py:67
  39.2 1.5 fusion.6
  40.8 1.6 fusion.8
  42.3 4.9 %gather_fusion.1 = bf16[128,4096]{1,0:T(8,128)(2,1)} fusion(bf16[2,64,4096]{2,1,0:T(8,128)(2,1)S(1)} %fusion.8, s32[128]{0:T(128)S(1)} %reshape.92), kind=kCustom, calls=%fused_computation.1 | custom fusion | bytes 2098176 | tf_op jit(solution)/shard_map/vmap()/gather | solution.py:78
  47.2 2.1 fusion.35
  49.3 4.8 %fusion.25 = bf16[2,8,8,8,128]{4,3,2,1,0:T(8,128)(2,1)S(1)} fusion(bf16[2,64,4096]{2,1,0:T(8,128)(2,1)S(1)} %bitcast.111, bf16[4096,1024]{1,0:T(8,128)(2,1)} %param.18), kind=kOutput, calls=%fused_computation.38 | convolution fusion | flops 1073872896 | bytes 9699328 | tf_op jit(solution)/shard_map/bmd,dc->bmc/dot_general | solution.py:80
  56.8 1.7 slice-done.1
  58.4 2.6 fusion
  61.3 1.0 copy-done.2
  62.3 4.9 %gather_fusion = bf16[128,4096]{1,0:T(8,128)(2,1)} fusion(bf16[2,64,4096]{2,1,0:T(8,128)(2,1)S(1)} %copy-done.2, s32[128]{0:T(128)S(1)} %reshape.92), kind=kCustom, calls=%fused_computation | custom fusion | bytes 2098176 | tf_op jit(solution)/shard_map/vmap()/gather | solution.py:77
  67.1 63.7 %all-reduce.2.cloned.1.call-done = f32[2,64,4096]{2,1,0:T(8,128)} async-done(((f32[2,64,4096]{2,1,0:T(8,128)}), f32[2,64,4096]{2,1,0:T(8,128)}) %all-reduce.2.cloned.1.call-update) | async-done | bytes 2097168 | tf_op jit(solution)/shard_map/psum | solution.py:113
  130.9 2.4 multiply_reduce_fusion
  133.3 1.3 copy-done.3
  135.1 4.9 %fusion.9 = f32[2,64,4096]{2,1,0:T(8,128)} fusion(bf16[256,4096]{1,0:T(8,128)(2,1)S(1)} %copy-done, bf16[4096,256]{1,0:T(8,128)(2,1)} %param.22, f32[2,64,4096]{2,1,0:T(8,128)} %copy-done.3, f32[4096]{0:T(1024)S(1)} %copy-done.8, f32[2,64]{1,0:T(2,128)S(1)} %add_rsqrt_fusion.1, f32[2,64,256]{2,1,0:T(8,128)S(1)} %fusion.13), kind=kOutput, calls=%fused_computation.15 | convolution fusion | flops 538640384 | bytes 8536576 | tf_op jit(solution)/shard_map/bmc,cd->bmd/dot_general | solution.py:120
  140.1 0.8 dynamic_slice.20
  140.9 34.4 %reduce-scatter.2.cloned.1.call-done = f32[2,64,1024]{2,1,0:T(8,128)} async-done(((f32[2,64,4096]{2,1,0:T(8,128)}), f32[2,64,1024]{2,1,0:T(8,128)}) %reduce-scatter.2.cloned.1.call-update) | async-done | bytes 524304 | tf_op jit(solution)/shard_map/reduce_scatter | solution.py:123
  175.4 1.2 multiply_reduce_fusion.1
  176.5 8.9 %psum.22 = f32[2,64]{1,0:T(2,128)S(1)} all-reduce(f32[2,64]{1,0:T(2,128)S(1)} %multiply_reduce_fusion.1), channel_id=1, replica_groups=mesh['wide'=8,'narrow'=4] {'narrow'}, use_global_device_ids=true, to_apply=%region_9.10 | all-reduce | flops 128 | bytes 1024 | tf_op jit(solution)/shard_map/psum | solution.py:125
  185.5 1.2 multiply_multiply_fusion
  186.7 2.5 collective-permute-start
  189.1 10.2 %collective-permute-done = f32[1,64,1024]{2,1,0:T(8,128)S(1)} collective-permute-done((f32[1,64,1024]{2,1,0:T(8,128)S(1)}, f32[1,64,1024]{2,1,0:T(8,128)S(1)}, u32[]{:S(2)}, u32[]{:S(2)}) %collective-permute-start) | collective-permute-done | bytes 262176 | tf_op jit(solution)/shard_map/ppermute | solution.py:20
  199.3 0.7 add_convert_fusion
  200.1 22.1 %all-gather.8.cloned.1.call-done = bf16[1,512,1024]{2,1,0:T(8,128)(2,1)} async-done(((bf16[1,64,1024]{2,1,0:T(8,128)(2,1)}), bf16[1,512,1024]{2,1,0:T(8,128)(2,1)}) %all-gather.8.cloned.1.call-update) | async-done | bytes 1048592 | tf_op jit(solution)/shard_map/all_gather | solution.py:131
  222.3 54.0 %all-gather.10.cloned.1.call-done = bf16[1,512,4096]{2,1,0:T(8,128)(2,1)} async-done(((bf16[1,512,1024]{2,1,0:T(8,128)(2,1)}), bf16[1,512,4096]{2,1,0:T(8,128)(2,1)}) %all-gather.10.cloned.1.call-update) | async-done | bytes 4194320 | tf_op jit(solution)/shard_map/all_gather | solution.py:133
  276.3 8.1 %fusion.4 = f32[512,1024]{1,0:T(8,128)S(1)} fusion(bf16[4096,1024]{1,0:T(8,128)(2,1)} %param.24, bf16[1,512,4096]{2,1,0:T(8,128)(2,1)} %all-gather.10.cloned.1.call-done), kind=kOutput, calls=%fused_computation.6 | convolution fusion | flops 4294967296 | bytes 14680064 | tf_op jit(solution)/shard_map/dot_general | solution.py:132
  284.4 1.6 copy.39
  286.3 39.3 %pmax.7 = f32[512]{0:T(512)S(1)} all-reduce(f32[512]{0:T(512)S(1)} %reduce_max.32), channel_id=1, replica_groups=mesh['wide'=8,'narrow'=4] {'wide','narrow'}, use_global_device_ids=true, to_apply=%region_11.12 | all-reduce | flops 512 | bytes 4096 | tf_op jit(solution)/shard_map/pmax | solution.py:140
  326.3 40.9 %psum.23 = f32[512]{0:T(512)S(1)} all-reduce(f32[512]{0:T(512)S(1)} %reduce_sum.62), channel_id=1, replica_groups=mesh['wide'=8,'narrow'=4] {'wide','narrow'}, use_global_device_ids=true, to_apply=%region_13.14 | all-reduce | flops 512 | bytes 4096 | tf_op jit(solution)/shard_map/psum | solution.py:141
  367.9 3.3 bitcast_subtract_fusion
  (59 shorter events, 6.1 us)
Async XLA Ops:
  7.2 127.9 %copy-start = (bf16[256,4096]{1,0:T(8,128)(2,1)S(1)}, bf16[256,4096]{1,0:T(8,128)(2,1)}, u32[]{:S(2)}) copy-start(bf16[256,4096]{1,0:T(8,128)(2,1)} %param.23) | copy-start | bytes 6291460
  7.2 5.2 %copy-start.10 = (s32[2]{0:T(128)S(1)}, s32[2]{0:T(128)}, u32[]{:S(2)}) copy-start(s32[2]{0:T(128)} %param.26) | copy-start | bytes 28
  7.2 32.0 %all-gather.6.cloned.1.call-start = ((), (), s32[]{:S(2)}) async-start(), calls=%async_computation.1 | async-start | bytes 1310720 | tf_op jit(solution)/shard_map/all_gather | solution.py:67
  7.9 122.9 %all-reduce.2.cloned.1.call-start = ((), (), s32[]{:S(2)}) async-start(), calls=%async_computation.2 | async-start | bytes 4194304 | tf_op jit(solution)/shard_map/psum | solution.py:113
  8.8 32.0 %copy-start.9 = (f32[4096]{0:T(1024)S(1)}, f32[4096]{0:T(1024)}, u32[]{:S(2)}) copy-start(f32[4096]{0:T(1024)} %param.15) | copy-start | bytes 49156
  47.2 2.2 copy-start.5
  49.3 5.2 %copy-start.7 = (bf16[2,512,1,256]{3,1,0,2:T(8,128)(2,1)S(1)}, bf16[2,512,1,256]{3,1,0,2:T(8,128)(2,1)}, u32[]{:S(2)}) copy-start(bf16[2,512,1,256]{3,1,0,2:T(8,128)(2,1)} %copy.68) | copy-start | bytes 1572868
  54.5 2.2 slice-start
  56.1 2.3 slice-start.1
  61.0 1.2 copy-start.2
  61.1 114.3 %reduce-scatter.2.cloned.1.call-start = ((), (), s32[]{:S(2)}) async-start(), calls=%async_computation.3 | async-start | bytes 2621440 | tf_op jit(solution)/shard_map/reduce_scatter | solution.py:123
  130.9 3.7 copy-start.6
  130.9 3.7 copy-start.8
  133.2 1.3 copy-start.3
  140.0 35.4 %copy-start.4 = (f32[2,64,4096]{2,1,0:T(8,128)S(1)}, f32[2,64,4096]{2,1,0:T(8,128)}, u32[]{:S(2)}) copy-start(f32[2,64,4096]{2,1,0:T(8,128)} %copy-done.3) | copy-start | bytes 6291460
  140.0 82.2 %all-gather.8.cloned.1.call-start = ((), (), s32[]{:S(2)}) async-start(), calls=%async_computation.4 | async-start | bytes 1179648 | tf_op jit(solution)/shard_map/all_gather | solution.py:131
  186.7 12.6 %collective-permute-start = (f32[1,64,1024]{2,1,0:T(8,128)S(1)}, f32[1,64,1024]{2,1,0:T(8,128)S(1)}, u32[]{:S(2)}, u32[]{:S(2)}) collective-permute-start(f32[1,64,1024]{2,1,0:T(8,128)S(1)} %slice_select_fusion), channel_id=1, source_target_pairs={{0,16},{4,20},{8,24},{12,28},{16,0},{20,4},{24,8},{28,12},{1,17},{... | collective-permute-start | bytes 786440 | tf_op jit(solution)/shard_map/ppermute | solution.py:20
  200.1 76.2 %all-gather.10.cloned.1.call-start = ((), (), s32[]{:S(2)}) async-start(), calls=%async_computation.5 | async-start | bytes 5242880 | tf_op jit(solution)/shard_map/all_gather | solution.py:133
  367.9 3.3 copy-start.1
Sparse Core Ops, SparseCore 0:
  9.9 29.3 all-gather.5
  61.2 69.6 all-reduce.1
  140.2 35.1 reduce-scatter.1
  200.2 22.0 all-gather.7
  223.9 52.3 all-gather.9
where the time goes:
time: 378 us
  waiting for transfers between devices  212 us (56%)
  blocking collectives  89.2 us (24%)
  matrix products  24.9 us (7%)
  local copies, waits for them, and re-layouts  20.7 us (5%)
  other arithmetic  14 us (4%)
  between operations  14 us (4%)
    psum x1, waiting for transfers between devices, on_device(): attn_total = lax.psum(attn_part, 'narrow')  63.7 us
    all_gather x1, waiting for transfers between devices, on_device(): lax.all_gather(all_rows, 'narrow', axis=1, tiled=True)  54 us
    psum x1, blocking collectives, on_device(): lax.psum(jnp.sum(jnp.exp(logits - row_peak[:, None]), axis=-1), ('wide',...  40.9 us
    pmax x1, blocking collectives, on_device(): row_peak = lax.pmax(local_peak, ('wide', 'narrow'))  39.3 us
    reduce_scatter x1, waiting for transfers between devices, on_device(): lax.psum_scatter(ffn_part, 'narrow', scatter_dimension=2, tiled=True)  34.4 us
    all_gather x1, waiting for transfers between devices, on_device(): full_rows = lax.all_gather(block_states, 'narrow', axis=2, tiled=True)  26.8 us
    all_gather x1, waiting for transfers between devices, on_device(): all_rows = lax.all_gather(guided, 'wide', axis=0, tiled=True)  22.1 us
    ppermute x1, waiting for transfers between devices, swapped(): return lax.ppermute(value, axis, pairs)  10.2 us
  transfers between devices with their start and end apart: 6, of which 6 were waited for; matrix products, arithmetic and copies ran while one was open for 3% of the time, Pallas kernels for 0%

commit v1 on v0

v1 whole, which is shorter than its diff:
```python
import functools
import math

import jax
import jax.numpy as jnp
from jax import lax
from jax.experimental import pallas as pl
from jax.experimental.pallas import tpu as pltpu
from jax.sharding import PartitionSpec as P

KVH = 4
HD = 128
EPS = 1e-06
GUIDE = 1.5
CHUNKS = 4
MESH = pl.DeviceIdType.MESH
F32 = jnp.float32
BF16 = jnp.bfloat16


def dot(a, b):
    return jnp.dot(a, b, preferred_element_type=F32)


def push(src, dst, send, recv, where):
    return pltpu.make_async_remote_copy(
        src_ref=src, dst_ref=dst, send_sem=send, recv_sem=recv, device_id=where, device_id_type=MESH
    )


def greet(others):
    barrier = pltpu.get_barrier_semaphore()
    for where in others:
        pl.semaphore_signal(barrier, inc=1, device_id=where, device_id_type=MESH)
    pl.semaphore_wait(barrier, len(others))


def gather_kernel(n_narrow, mine, gain, full_out, normed_out, full, send, recv, local):
    n = lax.axis_index("narrow")
    w = lax.axis_index("wide")
    cols = mine.shape[1]
    others = [{"wide": w, "narrow": lax.rem(n + d, n_narrow)} for d in range(1, n_narrow)]
    span = pl.ds(pl.multiple_of(n * cols, cols), cols)
    keep = pltpu.make_async_copy(mine, full.at[:, span], local)
    keep.start()
    greet(others)
    copies = [
        push(mine, full.at[:, span], send.at[d], recv.at[d], where) for d, where in enumerate(others)
    ]
    for copy in copies:
        copy.start()
    keep.wait()
    for copy in copies:
        copy.wait()

    rows = full.shape[0]
    step = 16

    def norm_rows(i, carry):
        at = pl.ds(pl.multiple_of(i * step, step), step)
        raw = full[at, :]
        value = raw.astype(F32)
        full_out[at, :] = raw
        scale = lax.rsqrt(jnp.mean(value * value, axis=-1, keepdims=True) + EPS)
        normed_out[at, :] = (value * scale * gain[...]).astype(BF16)
        return carry

    lax.fori_loop(0, rows // step, norm_rows, 0)


def gather_rows(n_narrow, mine, gain):
    rows, cols = mine.shape
    shape = jax.ShapeDtypeStruct((rows, cols * n_narrow), BF16)
    vmem = pl.BlockSpec(memory_space=pltpu.VMEM)
    return pl.pallas_call(
        functools.partial(gather_kernel, n_narrow),
        out_shape=(shape, shape),
        in_specs=[vmem, vmem],
        out_specs=(vmem, vmem),
        scratch_shapes=[
            pltpu.VMEM(shape.shape, BF16),
            pltpu.SemaphoreType.DMA((n_narrow - 1,)),
            pltpu.SemaphoreType.DMA((n_narrow - 1,)),
            pltpu.SemaphoreType.DMA,
        ],
        compiler_params=pltpu.CompilerParams(
            collective_id=0, has_side_effects=True, vmem_limit_bytes=24 * 2**20
        ),
    )(mine, gain)


def tail_kernel(
    n_wide,
    n_narrow,
    attended,
    picked,
    ffn_gain,
    final_gain,
    w_out,
    w_gate,
    w_up,
    w_down,
    w_head,
    logits,
    stats,
    wo,
    wg,
    wu,
    wd,
    wh,
    part,
    sent_a,
    sent_b,
    got_a,
    got_b,
    first,
    ffn_in,
    gate_acc,
    up_acc,
    swap_out,
    swap_in,
    guided,
    row_peak,
    row_total,
    board,
    load_sem,
    rs_send,
    rs_recv,
    ag_send,
    ag_recv,
    rt_send,
    rt_recv,
    swap_sem,
    z_send,
    z_recv,
    n_send,
    n_recv,
    s_send,
    s_recv,
    st_send,
    st_recv,
):
    n = lax.axis_index("narrow")
    w = lax.axis_index("wide")
    half = n_wide // 2
    pairs = n_wide // 2
    rows, width = ffn_in.shape
    mine = rows // n_narrow
    chunk = width // CHUNKS
    near = [lax.rem(n + d, n_narrow) for d in range(n_narrow)]
    far = [lax.rem(w + 2 * k, n_wide) for k in range(pairs)]
    twin = w + 1 - 2 * lax.rem(w, 2)
    near_at = [{"wide": w, "narrow": i} for i in near]
    far_at = [{"wide": i, "narrow": n} for i in far]
    twin_at = {"wide": twin, "narrow": n}

    def cols(c):
        return pl.ds(pl.multiple_of(c * chunk, chunk), chunk)

    def block_rows(i):
        return pl.ds(pl.multiple_of(i * mine, mine), mine)

    own = block_rows(n)
    loads = [
        pltpu.make_async_copy(w_out.at[:, cols(c)], wo.at[:, cols(c)], load_sem.at[c])
        for c in range(CHUNKS)
    ]
    for i, (src, dst) in enumerate(((w_gate, wg), (w_up, wu), (w_down, wd), (w_head, wh))):
        loads.append(pltpu.make_async_copy(src, dst, load_sem.at[CHUNKS + i]))
    for load in loads:
        load.start()
    greet(near_at[1:] + far_at[1:] + [twin_at])

    def scatter(sent, got, send, recv, c):
        return [
            push(
                sent.at[block_rows(near[d]), cols(c)],
                got.at[d - 1, :, cols(c)],
                send.at[c, d - 1],
                recv.at[c, d - 1],
                near_at[d],
            )
            for d in range(1, n_narrow)
        ]

    for c in range(CHUNKS):
        loads[c].wait()
        value = dot(attended[...], wo[:, cols(c)])
        part[:, cols(c)] = value
        sent_a[:, cols(c)] = value.astype(BF16)
        for copy in scatter(sent_a, got_a, rs_send, rs_recv, c):
            copy.start()
    square = jnp.zeros((mine, 1), F32)
    for c in range(CHUNKS):
        for copy in scatter(sent_a, got_a, rs_send, rs_recv, c):
            copy.wait_recv()
        value = picked[:, cols(c)].astype(F32) + part[own, cols(c)]
        for d in range(n_narrow - 1):
            value = value + got_a[d, :, cols(c)].astype(F32)
        first[:, cols(c)] = value
        square = square + jnp.sum(value * value, axis=-1, keepdims=True)
    scale = lax.rsqrt(square / width + EPS)

    def spread(c):
        return [
            push(
                ffn_in.at[own, cols(c)],
                ffn_in.at[own, cols(c)],
                ag_send.at[c, d - 1],
                ag_recv.at[c, d - 1],
                near_at[d],
            )
            for d in range(1, n_narrow)
        ]

    for c in range(CHUNKS):
        ffn_in[own, cols(c)] = (first[:, cols(c)] * scale * ffn_gain[:, cols(c)]).astype(BF16)
        for copy in spread(c):
            copy.start()
    for load in loads[CHUNKS : CHUNKS + 3]:
        load.wait()
    for c in range(CHUNKS):
        for copy in spread(c):
            copy.wait_recv()
        gate_part = dot(ffn_in[:, cols(c)], wg[cols(c), :])
        up_part = dot(ffn_in[:, cols(c)], wu[cols(c), :])
        if c == 0:
            gate_acc[...] = gate_part
            up_acc[...] = up_part
        else:
            gate_acc[...] += gate_part
            up_acc[...] += up_part
    gate = gate_acc[...]
    hidden = (gate / (1.0 + jnp.exp(-gate)) * up_acc[...]).astype(BF16)

    for c in range(CHUNKS):
        value = dot(hidden, wd[:, cols(c)])
        part[:, cols(c)] = value
        sent_b[:, cols(c)] = value.astype(BF16)
        for copy in scatter(sent_b, got_b, rt_send, rt_recv, c):
            copy.start()
    square = jnp.zeros((mine, 1), F32)
    for c in range(CHUNKS):
        for copy in scatter(sent_b, got_b, rt_send, rt_recv, c):
            copy.wait_recv()
        value = first[:, cols(c)] + part[own, cols(c)]
        for d in range(n_narrow - 1):
            value = value + got_b[d, :, cols(c)].astype(F32)
        first[:, cols(c)] = value
        square = square + jnp.sum(value * value, axis=-1, keepdims=True)
    scale = lax.rsqrt(square / width + EPS)
    first[...] = first[...] * scale * final_gain[...]

    upper = w // half
    wide_half = width // 2

    def side(i):
        return pl.ds(pl.multiple_of(i * wide_half, wide_half), wide_half)

    swap_out[...] = first[:, side(1 - upper)].astype(BF16)
    swap = push(
        swap_out,
        swap_in,
        swap_sem.at[0],
        swap_sem.at[1],
        {"wide": lax.rem(w + half, n_wide), "narrow": n},
    )
    swap.start()

    def region(source, narrow):
        start = lax.rem(source, half) * rows + narrow * mine
        return guided.at[pl.ds(pl.multiple_of(start, mine), mine), side(source // half)]

    swap.wait()
    kept = first[:, side(upper)]
    other = swap_in[...].astype(F32)
    cond = jnp.where(upper == 1, other, kept)
    uncond = jnp.where(upper == 1, kept, other)
    region(w, n)[...] = (uncond + GUIDE * (cond - uncond)).astype(BF16)

    def from_far(k):
        return lax.rem(w + n_wide - 2 * k, n_wide)

    def from_near(d):
        return lax.rem(n + n_narrow - d, n_narrow)

    def z_copy(k):
        spot = region(w, n)
        return push(spot, spot, z_send.at[k], z_recv.at[k], far_at[k])

    def n_copy(k, d):
        spot = region(from_far(k), n)
        return push(spot, spot, n_send.at[k, d], n_recv.at[k, d], near_at[d])

    def s_copy(k, d):
        spot = region(from_far(k), from_near(d))
        return push(spot, spot, s_send.at[k, d], s_recv.at[k, d], twin_at)

    for k in range(1, pairs):
        z_copy(k).start()
    for k in range(pairs):
        if k:
            z_copy(k).wait_recv()
        for d in range(1, n_narrow):
            n_copy(k, d).start()
        s_copy(k, 0).start()
    for k in range(pairs):
        for d in range(1, n_narrow):
            n_copy(k, d).wait_recv()
            s_copy(k, d).start()
    for k in range(pairs):
        for d in range(n_narrow):
            s_copy(k, d).wait_recv()

    loads[CHUNKS + 3].wait()
    tile = 256

    def logit_tile(j, carry):
        at = pl.ds(pl.multiple_of(j * tile, tile), tile)
        logits[:, at] = dot(guided[...], wh[:, at])
        return carry

    lax.fori_loop(0, logits.shape[1] // tile, logit_tile, 0)
    step = 64

    def row_stats(i, carry):
        at = pl.ds(pl.multiple_of(i * step, step), step)
        value = logits[at, :]
        top = jnp.max(value, axis=-1, keepdims=True)
        total = jnp.sum(jnp.exp(value - top), axis=-1, keepdims=True)
        row_peak[at, :] = jnp.broadcast_to(top, (step, row_peak.shape[1]))
        row_total[at, :] = jnp.broadcast_to(total, (step, row_peak.shape[1]))
        return carry

    count = logits.shape[0]
    lax.fori_loop(0, count // step, row_stats, 0)
    peak = row_peak[...].T[0:1, :]
    total = row_total[...].T[0:1, :]

    slot = 0
    for stage, places in enumerate(([twin_at], near_at[1:], far_at[1:])):
        board[slot, :, 0:count] = peak
        board[slot, :, count:] = total
        copies = [
            push(
                board.at[slot],
                board.at[slot + 1 + i],
                st_send.at[slot + 1 + i],
                st_recv.at[slot + 1 + i],
                where,
            )
            for i, where in enumerate(places)
        ]
        for copy in copies:
            copy.start()
        for copy in copies:
            copy.wait()
        top = peak
        for i in range(len(places)):
            top = jnp.maximum(top, board[slot + 1 + i, :, 0:count])
        total = total * jnp.exp(peak - top)
        for i in range(len(places)):
            got = board[slot + 1 + i]
            total = total + got[:, count:] * jnp.exp(got[:, 0:count] - top)
        peak = top
        slot += 1 + len(places)
    stats[0:1, :] = peak + jnp.log(total)
    stats[1:2, :] = 1.0 / total

    for c in range(CHUNKS):
        for copy in scatter(sent_a, got_a, rs_send, rs_recv, c):
            copy.wait_send()
        for copy in scatter(sent_b, got_b, rt_send, rt_recv, c):
            copy.wait_send()
        for copy in spread(c):
            copy.wait_send()
    for k in range(pairs):
        if k:
            z_copy(k).wait_send()
        for d in range(n_narrow):
            if d:
                n_copy(k, d).wait_send()
            s_copy(k, d).wait_send()


def tail(n_wide, n_narrow, attended, picked, ffn_gain, final_gain, *weights):
    w_out, w_gate, w_up, w_down, w_head = weights
    rows = attended.shape[0]
    width = picked.shape[1]
    mine = rows // n_narrow
    pairs = n_wide // 2
    total_rows = rows * pairs
    vocab_cols = w_head.shape[1]
    vmem = pl.BlockSpec(memory_space=pltpu.VMEM)
    hbm = pl.BlockSpec(memory_space=pl.ANY)
    near = n_narrow - 1
    slots = 3 + 1 + near + pairs - 1
    dma = pltpu.SemaphoreType.DMA
    return pl.pallas_call(
        functools.partial(tail_kernel, n_wide, n_narrow),
        out_shape=(
            jax.ShapeDtypeStruct((total_rows, vocab_cols), F32),
            jax.ShapeDtypeStruct((2, total_rows), F32),
        ),
        in_specs=[vmem] * 4 + [hbm] * 5,
        out_specs=(vmem, vmem),
        scratch_shapes=[pltpu.VMEM(v.shape, BF16) for v in weights]
        + [
            pltpu.VMEM((rows, width), F32),
            pltpu.VMEM((rows, width), BF16),
            pltpu.VMEM((rows, width), BF16),
            pltpu.VMEM((near, mine, width), BF16),
            pltpu.VMEM((near, mine, width), BF16),
            pltpu.VMEM((mine, width), F32),
            pltpu.VMEM((rows, width), BF16),
            pltpu.VMEM((rows, w_gate.shape[1]), F32),
            pltpu.VMEM((rows, w_gate.shape[1]), F32),
            pltpu.VMEM((mine, width // 2), BF16),
            pltpu.VMEM((mine, width // 2), BF16),
            pltpu.VMEM((total_rows, width), BF16),
            pltpu.VMEM((total_rows, 128), F32),
            pltpu.VMEM((total_rows, 128), F32),
            pltpu.VMEM((slots, 1, 2 * total_rows), F32),
            dma((CHUNKS + 4,)),
            dma((CHUNKS, near)),
            dma((CHUNKS, near)),
            dma((CHUNKS, near)),
            dma((CHUNKS, near)),
            dma((CHUNKS, near)),
            dma((CHUNKS, near)),
            dma((2,)),
            dma((pairs,)),
            dma((pairs,)),
            dma((pairs, n_narrow)),
            dma((pairs, n_narrow)),
            dma((pairs, n_narrow)),
            dma((pairs, n_narrow)),
            dma((slots,)),
            dma((slots,)),
        ],
        compiler_params=pltpu.CompilerParams(
            collective_id=1, has_side_effects=True, vmem_limit_bytes=60 * 2**20
        ),
    )(attended, picked, ffn_gain, final_gain, *weights)


def on_device(
    block_states,
    attn_gain,
    ffn_gain,
    final_gain,
    w_query,
    w_keyval,
    w_out,
    w_gate,
    w_up,
    w_down,
    w_head,
    cache,
    prefix_lengths,
    masked_positions,
):
    n_wide = lax.axis_size("wide")
    n_narrow = lax.axis_size("narrow")
    wide_index = lax.axis_index("wide")
    narrow_index = lax.axis_index("narrow")
    half_wide = n_wide // 2
    local_req, block, _ = block_states.shape
    masked = masked_positions.shape[1]
    width = w_query.shape[0]

    full_rows, normed = gather_rows(
        n_narrow, block_states.reshape(local_req * block, -1), attn_gain[None, :]
    )
    full_rows = full_rows.reshape(local_req, block, width)

    kv_head = narrow_index // (n_narrow // KVH)
    head_weight = lax.dynamic_slice_in_dim(w_keyval, kv_head * (2 * HD), 2 * HD, 1)
    block_kv = dot(normed, head_weight).astype(BF16).reshape(local_req, block, 2 * HD)
    cache_kv = lax.dynamic_index_in_dim(cache, kv_head, axis=2, keepdims=False)
    first_req = wide_index % half_wide * local_req
    my_positions = lax.dynamic_slice_in_dim(masked_positions, first_req, local_req, 0)
    choose = (my_positions[:, :, None] == jnp.arange(block)[None, None, :]).astype(BF16)
    picked = jnp.einsum("bml,bld->bmd", choose, full_rows, preferred_element_type=F32)
    picked = picked.astype(BF16).reshape(local_req * masked, width)
    mine = local_req * masked // n_narrow
    picked = lax.dynamic_slice_in_dim(picked, narrow_index * mine, mine, 0)
    local_heads = w_query.shape[1] // HD
    query = dot(normed, w_query).astype(BF16).reshape(local_req, block, local_heads * HD)
    query = jnp.einsum("bml,bld->bmd", choose, query, preferred_element_type=F32).astype(BF16)
    query = query.reshape(local_req, masked, local_heads, HD)
    scale = 1.0 / math.sqrt(HD)
    pre_scores = (
        jnp.einsum("bmhd,bpd->bhmp", query, cache_kv[..., :HD], preferred_element_type=F32) * scale
    )
    live = jnp.arange(cache_kv.shape[1])[None, :] < prefix_lengths[:, None]
    pre_scores = jnp.where(live[:, None, None, :], pre_scores, -jnp.inf)
    blk_scores = (
        jnp.einsum("bmhd,bld->bhml", query, block_kv[..., :HD], preferred_element_type=F32) * scale
    )
    peak = jnp.maximum(
        jnp.max(pre_scores, axis=-1, keepdims=True), jnp.max(blk_scores, axis=-1, keepdims=True)
    )
    pre_weights = jnp.exp(pre_scores - peak)
    blk_weights = jnp.exp(blk_scores - peak)
    weight_total = jnp.sum(pre_weights, axis=-1, keepdims=True) + jnp.sum(
        blk_weights, axis=-1, keepdims=True
    )
    pre_probs = (pre_weights / weight_total).astype(BF16)
    blk_probs = (blk_weights / weight_total).astype(BF16)
    attended = jnp.einsum(
        "bhmp,bpd->bmhd", pre_probs, cache_kv[..., HD:], preferred_element_type=F32
    )
    attended = attended + jnp.einsum(
        "bhml,bld->bmhd", blk_probs, block_kv[..., HD:], preferred_element_type=F32
    )
    attended = attended.astype(BF16).reshape(local_req * masked, local_heads * HD)

    logits, stats = tail(
        n_wide,
        n_narrow,
        attended,
        picked,
        ffn_gain[None, :],
        final_gain[None, :],
        w_out,
        w_gate,
        w_up,
        w_down,
        w_head,
    )
    return logits - stats[0][:, None], stats[1].reshape(-1, masked)


def solution(mesh):
    in_specs = (
        P("wide", None, "narrow"),
        P(),
        P(),
        P(),
        P(None, "narrow"),
        P(),
        P("narrow", None),
        P(None, "narrow"),
        P(None, "narrow"),
        P("narrow", None),
        P(None, ("wide", "narrow")),
        P("wide", None, None, None),
        P("wide"),
        P(),
    )
    out_specs = (P(None, ("wide", "narrow")), P())
    return jax.shard_map(
        on_device, mesh=mesh, in_specs=in_specs, out_specs=out_specs, check_vma=False
    )
```

time: 378 us -> 130 us (0.34)
  waiting for transfers between devices: 212 us -> 0 us
  Pallas kernels: 0 us -> 114 us
  blocking collectives: 89.2 us -> 0 us
  matrix products: 24.9 us -> 5.92 us
  local copies, waits for them, and re-layouts: 20.7 us -> 5.17 us
  between operations: 14 us -> 0.79 us
  other arithmetic: 14 us -> 4.57 us
    pallas_call x0 -> x2, Pallas kernels: none -> 114 us  [the longest x1 96.3 us: tail(): pl.pallas_call(functools.partial(tail_kernel, n_wide, n_narrow), out_shap...]
    all_gather x3 -> x0, waiting for transfers between devices: 103 us -> none  [the longest x1 54 us: on_device(): lax.all_gather(all_rows, 'narrow', axis=1, tiled=True)]
    psum x1 -> x0, waiting for transfers between devices: 63.7 us -> none  [on_device(): attn_total = lax.psum(attn_part, 'narrow')]
    psum x2 -> x0, blocking collectives: 49.9 us -> none  [the longest x1 40.9 us: on_device(): lax.psum(jnp.sum(jnp.exp(logits - row_peak[:, None]), axis=-1), ('wide',...]
    pmax x1 -> x0, blocking collectives: 39.3 us -> none  [on_device(): row_peak = lax.pmax(local_peak, ('wide', 'narrow'))]
    reduce_scatter x1 -> x0, waiting for transfers between devices: 34.4 us -> none  [on_device(): lax.psum_scatter(ffn_part, 'narrow', scatter_dimension=2, tiled=True)]
    dot_general x6 -> x4, matrix products: 23.1 us -> 4.07 us  [the longest x2 3.32 us: dot(): return jnp.dot(a, b, preferred_element_type=F32)]
    ppermute x1 -> x0, waiting for transfers between devices: 10.2 us -> none  [swapped(): return lax.ppermute(value, axis, pairs)]
  transfers between devices with their start and end apart: 6 -> 0, of which waited for: 6 -> 0; matrix products, arithmetic and copies ran while one was open for 3% -> 0% of each run, Pallas kernels for 0% -> 0%
where the time goes in v1:
time: 130 us
  Pallas kernels  114 us (88%)
  matrix products  5.92 us (5%)
  local copies, waits for them, and re-layouts  5.17 us (4%)
  other arithmetic  4.57 us (4%)
    pallas_call x1, Pallas kernels, tail(): pl.pallas_call(functools.partial(tail_kernel, n_wide, n_narrow), out_shap...  96.3 us
    pallas_call x1, Pallas kernels, gather_rows(): pl.pallas_call(functools.partial(gather_kernel, n_narrow), out_shape=(sha...  17.5 us
    dot_general x2, matrix products, dot(): return jnp.dot(a, b, preferred_element_type=F32)  3.32 us
    sub x1, other arithmetic, on_device(): return (logits - stats[0][:, None], stats[1].reshape(-1, masked))  3.11 us

profile of v1, /device:TPU:0, one launch (start us, length us, event | category | flops | bytes accessed | tf_op | source)
XLA Modules:
  0.0 130.2 jit_solution(264011159075419592)
XLA Ops:
  0.6 0.0 copy-start
  0.6 0.0 copy-start.2
  0.7 0.0 copy-start.1
  0.7 0.8 constant_dynamic-slice_fusion.1
  1.5 0.7 iota_compare_fusion.3
  2.3 0.0 copy-done
  2.3 0.0 copy-start.3
  2.3 1.1 constant_dynamic-slice_fusion.2
  3.3 0.1 copy.47
  3.4 0.0 copy-done.2
  3.5 0.0 copy-done.1
  3.5 17.5 %shard_map.149 = (bf16[128,4096]{1,0:T(8,128)(2,1)S(1)}, bf16[128,4096]{1,0:T(8,128)(2,1)S(1)}) custom-call(bf16[128,1024]{1,0:T(8,128)(2,1)S(1)} %bitcast.72, f32[1,4096]{1,0:T(1,128)S(1)} %bitcast.73), custom_call_target="tpu_custom_call" | custom-call | tf_op jit(solution)/shard_map/pallas_call | solution.py:75
  20.9 0.5 convolution_convert_fusion
  21.4 0.8 constant_dynamic-slice_fusion.picked
  22.2 2.1 %fusion.8 = bf16[128,256]{1,0:T(8,128)(2,1)S(1)} fusion(bf16[128,4096]{1,0:T(8,128)(2,1)S(1)} %get-tuple-element.6, bf16[4096,1024]{1,0:T(8,128)(2,1)} %param.19, s32[]{:T(128)S(6)} %select_n.34), kind=kOutput, calls=%fused_computation.17 | convolution fusion | flops 268468224 | bytes 3211268 | tf_op jit(solution)/shard_map/dot_general | solution.py:22
  24.2 0.0 copy-done.3
  24.2 1.3 convolution_convert_fusion.2
  25.5 0.3 fusion.6
  25.8 0.4 fusion.24
  26.2 0.5 bitcast_reduce_fusion
  26.7 0.1 fusion.12
  26.8 0.6 fusion.3
  27.5 0.3 fusion.16
  27.7 0.7 fusion.7
  28.4 0.2 copy.24
  28.6 0.8 copy.48
  29.3 96.3 %shard_map.150 = (f32[512,1024]{1,0:T(8,128)}, f32[2,512]{1,0:T(2,128)}) custom-call(bf16[128,1024]{1,0:T(8,128)(2,1)} %bitcast.77, bf16[32,4096]{1,0:T(8,128)(2,1)} %constant_dynamic-slice_fusion.picked, f32[1,4096]{1,0:T(1,128)} %bitcast.82, f32[1,4096]{1,0:T(1,128)} %bitcast.83, bf16[1024,4096]{1,0:T(8,128)(2,1)} %w_out.1, bf16[4096,256]{1,0:T(8,128)(2,1)} %w_gate.1, ...), custom_call_target="tpu_custom_call" | custom-call | tf_op jit(solution)/shard_map/pallas_call | solution.py:399
  125.7 0.8 slice_reduce_fusion
  126.4 3.1 %broadcast_subtract_fusion = f32[512,1024]{1,0:T(8,128)} fusion(f32[512,1024]{1,0:T(8,128)} %get-tuple-element.8, f32[512]{0:T(512)S(1)} %bitcast.84), kind=kLoop, calls=%fused_computation.18 | loop fusion | flops 524288 | bytes 4196352 | tf_op jit(solution)/shard_map/sub | solution.py:532
  129.5 0.7 reshape_squeeze.3
  (2 shorter events, 0.0 us)
Async XLA Ops:
  0.6 1.6 %copy-start = (bf16[2,512,4,256]{3,2,1,0:T(4,128)(2,1)S(1)}, bf16[2,512,4,256]{3,2,1,0:T(4,128)(2,1)}, u32[]{:S(2)}) copy-start(bf16[2,512,4,256]{3,2,1,0:T(4,128)(2,1)} %param.25) | copy-start | bytes 6291460
  0.6 2.8 %copy-start.2 = (f32[4096]{0:T(1024)S(1)}, f32[4096]{0:T(1024)}, u32[]{:S(2)}) copy-start(f32[4096]{0:T(1024)} %param.15) | copy-start | bytes 49156
  0.7 2.8 %copy-start.1 = (bf16[2,64,1024]{2,1,0:T(8,128)(2,1)S(1)}, bf16[2,64,1024]{2,1,0:T(8,128)(2,1)}, u32[]{:S(2)}) copy-start(bf16[2,64,1024]{2,1,0:T(8,128)(2,1)} %param.14) | copy-start | bytes 786436
  2.3 22.0 %copy-start.3 = (bf16[4096,1024]{1,0:T(8,128)(2,1)S(1)}, bf16[4096,1024]{1,0:T(8,128)(2,1)}, u32[]{:S(2)}) copy-start(bf16[4096,1024]{1,0:T(8,128)(2,1)} %param.18) | copy-start | bytes 25165828

commit v2 on v1

--- a/solution.py
+++ b/solution.py
@@ -13,6 +13,7 @@
 EPS = 1e-06
 GUIDE = 1.5
 CHUNKS = 4
+LANES = 128
 MESH = pl.DeviceIdType.MESH
 F32 = jnp.float32
 BF16 = jnp.bfloat16
@@ -119,6 +120,9 @@
     up_acc,
     swap_out,
     swap_in,
+    ffn_scale,
+    scale_out,
+    scale_in,
     guided,
     row_peak,
     row_total,
@@ -130,9 +134,12 @@
     ag_recv,
     rt_send,
     rt_recv,
-    swap_sem,
-    z_send,
-    z_recv,
+    swap_send,
+    swap_recv,
+    sc_send,
+    sc_recv,
+    l_send,
+    l_recv,
     n_send,
     n_recv,
     s_send,
@@ -153,6 +160,9 @@
     near_at = [{"wide": w, "narrow": i} for i in near]
     far_at = [{"wide": i, "narrow": n} for i in far]
     twin_at = {"wide": twin, "narrow": n}
+    cross_at = [{"wide": twin, "narrow": i} for i in near[1:]]
+    place = w // 2
+    line_at = {1: {"wide": lax.rem(w + 2, n_wide), "narrow": n}, -1: {"wide": lax.rem(w + n_wide - 2, n_wide), "narrow": n}}
 
     def cols(c):
         return pl.ds(pl.multiple_of(c * chunk, chunk), chunk)
@@ -169,15 +179,16 @@
         loads.append(pltpu.make_async_copy(src, dst, load_sem.at[CHUNKS + i]))
     for load in loads:
         load.start()
-    greet(near_at[1:] + far_at[1:] + [twin_at])
-
-    def scatter(sent, got, send, recv, c):
+    greet(near_at[1:] + far_at[1:] + [twin_at] + cross_at)
+
+    def scatter(sent, got, send, recv, i, c=None):
+        c = i if c is None else c
         return [
             push(
                 sent.at[block_rows(near[d]), cols(c)],
                 got.at[d - 1, :, cols(c)],
-                send.at[c, d - 1],
-                recv.at[c, d - 1],
+                send.at[i, d - 1],
+                recv.at[i, d - 1],
                 near_at[d],
             )
             for d in range(1, n_narrow)
@@ -190,17 +201,6 @@
         sent_a[:, cols(c)] = value.astype(BF16)
         for copy in scatter(sent_a, got_a, rs_send, rs_recv, c):
             copy.start()
-    square = jnp.zeros((mine, 1), F32)
-    for c in range(CHUNKS):
-        for copy in scatter(sent_a, got_a, rs_send, rs_recv, c):
-            copy.wait_recv()
-        value = picked[:, cols(c)].astype(F32) + part[own, cols(c)]
-        for d in range(n_narrow - 1):
-            value = value + got_a[d, :, cols(c)].astype(F32)
-        first[:, cols(c)] = value
-        square = square + jnp.sum(value * value, axis=-1, keepdims=True)
-    scale = lax.rsqrt(square / width + EPS)
-
     def spread(c):
         return [
             push(
@@ -213,10 +213,31 @@
             for d in range(1, n_narrow)
         ]
 
+    scales = [
+        push(
+            ffn_scale.at[own],
+            ffn_scale.at[own],
+            sc_send.at[d - 1],
+            sc_recv.at[d - 1],
+            near_at[d],
+        )
+        for d in range(1, n_narrow)
+    ]
+    square = jnp.zeros((mine, 1), F32)
     for c in range(CHUNKS):
-        ffn_in[own, cols(c)] = (first[:, cols(c)] * scale * ffn_gain[:, cols(c)]).astype(BF16)
+        for copy in scatter(sent_a, got_a, rs_send, rs_recv, c):
+            copy.wait_recv()
+        value = picked[:, cols(c)].astype(F32) + part[own, cols(c)]
+        for d in range(n_narrow - 1):
+            value = value + got_a[d, :, cols(c)].astype(F32)
+        first[:, cols(c)] = value
+        ffn_in[own, cols(c)] = (value * ffn_gain[:, cols(c)]).astype(BF16)
         for copy in spread(c):
             copy.start()
+        square = square + jnp.sum(value * value, axis=-1, keepdims=True)
+    ffn_scale[own, :] = jnp.broadcast_to(lax.rsqrt(square / width + EPS), (mine, LANES))
+    for copy in scales:
+        copy.start()
     for load in loads[CHUNKS : CHUNKS + 3]:
         load.wait()
     for c in range(CHUNKS):
@@ -230,87 +251,149 @@
         else:
             gate_acc[...] += gate_part
             up_acc[...] += up_part
-    gate = gate_acc[...]
-    hidden = (gate / (1.0 + jnp.exp(-gate)) * up_acc[...]).astype(BF16)
-
-    for c in range(CHUNKS):
+    for copy in scales:
+        copy.wait_recv()
+    row_scale = ffn_scale[:, 0:1]
+    gate = gate_acc[...] * row_scale
+    hidden = (gate / (1.0 + jnp.exp(-gate)) * (up_acc[...] * row_scale)).astype(BF16)
+
+    upper = w // half
+    half_chunks = CHUNKS // 2
+    order = [lax.rem((1 - upper) * half_chunks + i, CHUNKS) for i in range(CHUNKS)]
+    for i, c in enumerate(order):
         value = dot(hidden, wd[:, cols(c)])
         part[:, cols(c)] = value
         sent_b[:, cols(c)] = value.astype(BF16)
-        for copy in scatter(sent_b, got_b, rt_send, rt_recv, c):
+        for copy in scatter(sent_b, got_b, rt_send, rt_recv, i, c):
             copy.start()
+
+    partner_at = {"wide": lax.rem(w + half, n_wide), "narrow": n}
+
+    def swap(i):
+        at = pl.ds(i * chunk, chunk)
+        return push(
+            swap_out.at[:, at], swap_in.at[:, at], swap_send.at[i], swap_recv.at[i], partner_at
+        )
+
+    scale_swap = push(
+        scale_out, scale_in, swap_send.at[half_chunks], swap_recv.at[half_chunks], partner_at
+    )
     square = jnp.zeros((mine, 1), F32)
-    for c in range(CHUNKS):
-        for copy in scatter(sent_b, got_b, rt_send, rt_recv, c):
+    for i, c in enumerate(order):
+        for copy in scatter(sent_b, got_b, rt_send, rt_recv, i, c):
             copy.wait_recv()
         value = first[:, cols(c)] + part[own, cols(c)]
         for d in range(n_narrow - 1):
             value = value + got_b[d, :, cols(c)].astype(F32)
-        first[:, cols(c)] = value
+        if i < half_chunks:
+            swap_out[:, pl.ds(i * chunk, chunk)] = value.astype(BF16)
+            swap(i).start()
+        else:
+            first[:, cols(c)] = value
         square = square + jnp.sum(value * value, axis=-1, keepdims=True)
     scale = lax.rsqrt(square / width + EPS)
-    first[...] = first[...] * scale * final_gain[...]
-
-    upper = w // half
-    wide_half = width // 2
-
-    def side(i):
-        return pl.ds(pl.multiple_of(i * wide_half, wide_half), wide_half)
-
-    swap_out[...] = first[:, side(1 - upper)].astype(BF16)
-    swap = push(
-        swap_out,
-        swap_in,
-        swap_sem.at[0],
-        swap_sem.at[1],
-        {"wide": lax.rem(w + half, n_wide), "narrow": n},
-    )
-    swap.start()
-
-    def region(source, narrow):
+    scale_out[...] = jnp.broadcast_to(scale, (mine, LANES))
+    scale_swap.start()
+
+    def region(source, narrow, i):
         start = lax.rem(source, half) * rows + narrow * mine
-        return guided.at[pl.ds(pl.multiple_of(start, mine), mine), side(source // half)]
-
-    swap.wait()
-    kept = first[:, side(upper)]
-    other = swap_in[...].astype(F32)
-    cond = jnp.where(upper == 1, other, kept)
-    uncond = jnp.where(upper == 1, kept, other)
-    region(w, n)[...] = (uncond + GUIDE * (cond - uncond)).astype(BF16)
-
-    def from_far(k):
-        return lax.rem(w + n_wide - 2 * k, n_wide)
+        return guided.at[
+            pl.ds(pl.multiple_of(start, mine), mine), cols(source // half * half_chunks + i)
+        ]
+
+    scale_swap.wait()
+    for i in range(half_chunks):
+        swap(i).wait()
+        c = order[half_chunks + i]
+        gain = final_gain[:, cols(c)]
+        kept = first[:, cols(c)] * scale * gain
+        other = swap_in[:, pl.ds(i * chunk, chunk)].astype(F32) * scale_in[:, 0:1] * gain
+        cond = jnp.where(upper == 1, other, kept)
+        uncond = jnp.where(upper == 1, kept, other)
+        region(w, n, i)[...] = (uncond + GUIDE * (cond - uncond)).astype(BF16)
+
+    parity = lax.rem(w, 2)
 
     def from_near(d):
         return lax.rem(n + n_narrow - d, n_narrow)
 
-    def z_copy(k):
-        spot = region(w, n)
-        return push(spot, spot, z_send.at[k], z_recv.at[k], far_at[k])
-
-    def n_copy(k, d):
-        spot = region(from_far(k), n)
-        return push(spot, spot, n_send.at[k, d], n_recv.at[k, d], near_at[d])
-
-    def s_copy(k, d):
-        spot = region(from_far(k), from_near(d))
-        return push(spot, spot, s_send.at[k, d], s_recv.at[k, d], twin_at)
-
-    for k in range(1, pairs):
-        z_copy(k).start()
-    for k in range(pairs):
-        if k:
-            z_copy(k).wait_recv()
+    def near_copy(i, j, d):
+        s = place + j
+        spot = region(2 * s + parity, n, i)
+        return push(spot, spot, n_send.at[i, s, d], n_recv.at[i, s, d], near_at[d])
+
+    def line_copy(route, j, step):
+        spot = region(2 * (place + j) + parity, from_near(route % n_narrow), route // n_narrow)
+        s = place + j
+        way = (step + 1) // 2
+        return push(
+            spot, spot, l_send.at[route, s, way], l_recv.at[route, s, way], line_at[step]
+        )
+
+    def twin_copy(i, j, d):
+        spot = region(2 * (place + j) + parity, from_near(d), i)
+        s = place + j
+        return push(spot, spot, s_send.at[i, s, d], s_recv.at[i, s, d], twin_at)
+
+    def there(j):
+        return jnp.logical_and(place + j >= 0, place + j < pairs)
+
+    def line_go(route, j, act):
+        for step in (1, -1):
+            if j * step <= 0:
+                pl.when(jnp.logical_and(there(j), there(step)))(
+                    lambda step=step: act(line_copy(route, j, step))
+                )
+
+    def line_take(route, j):
+        line_copy(route, j, -1 if j > 0 else 1).wait_recv()
+
+    def start(copy):
+        copy.start()
+
+    def all_near(j, act):
         for d in range(1, n_narrow):
-            n_copy(k, d).start()
-        s_copy(k, 0).start()
-    for k in range(pairs):
+            act(near_copy(0, j, d))
+
+    routes = [0] + [n_narrow + d for d in range(n_narrow)]
+    line_go(0, 0, start)
+    for d in range(1, n_narrow):
+        near_copy(1, 0, d).start()
+    line_go(n_narrow, 0, start)
+    all_near(0, start)
+    twin_copy(0, 0, 0).start()
+    twin_copy(1, 0, 0).start()
+    for d in range(1, n_narrow):
+        near_copy(1, 0, d).wait_recv()
+        line_go(n_narrow + d, 0, start)
+        twin_copy(1, 0, d).start()
+
+    def near_take(j):
         for d in range(1, n_narrow):
-            n_copy(k, d).wait_recv()
-            s_copy(k, d).start()
-    for k in range(pairs):
-        for d in range(n_narrow):
-            s_copy(k, d).wait_recv()
+            near_copy(0, j, d).wait_recv()
+            twin_copy(0, j, d).start()
+
+    near_take(0)
+    for reach in range(1, pairs):
+        for j in (-reach, reach):
+
+            def arrive(j=j):
+                line_take(0, j)
+                line_go(0, j, start)
+                all_near(j, start)
+                twin_copy(0, j, 0).start()
+                for d in range(n_narrow):
+                    line_take(n_narrow + d, j)
+                    line_go(n_narrow + d, j, start)
+                    twin_copy(1, j, d).start()
+
+            pl.when(there(j))(arrive)
+        for j in (-reach, reach):
+            pl.when(there(j))(functools.partial(near_take, j))
+    for i in range(half_chunks):
+        for s in range(pairs):
+            for d in range(n_narrow):
+                twin_copy(i, s - place, d).wait_recv()
 
     loads[CHUNKS + 3].wait()
     tile = 256
@@ -338,7 +421,7 @@
     total = row_total[...].T[0:1, :]
 
     slot = 0
-    for stage, places in enumerate(([twin_at], near_at[1:], far_at[1:])):
+    for stage, places in enumerate(([twin_at] + near_at[1:] + cross_at, far_at[1:])):
         board[slot, :, 0:count] = peak
         board[slot, :, count:] = total
         copies = [
@@ -367,20 +450,30 @@
     stats[0:1, :] = peak + jnp.log(total)
     stats[1:2, :] = 1.0 / total
 
-    for c in range(CHUNKS):
-        for copy in scatter(sent_a, got_a, rs_send, rs_recv, c):
+    for copy in scales:
+        copy.wait_send()
+    for i, c in enumerate(order):
+        for copy in scatter(sent_a, got_a, rs_send, rs_recv, i):
             copy.wait_send()
-        for copy in scatter(sent_b, got_b, rt_send, rt_recv, c):
+        for copy in scatter(sent_b, got_b, rt_send, rt_recv, i, c):
             copy.wait_send()
-        for copy in spread(c):
+        for copy in spread(i):
             copy.wait_send()
-    for k in range(pairs):
-        if k:
-            z_copy(k).wait_send()
-        for d in range(n_narrow):
-            if d:
-                n_copy(k, d).wait_send()
-            s_copy(k, d).wait_send()
+
+    def sent(copy):
+        copy.wait_send()
+
+    for d in range(1, n_narrow):
+        near_copy(1, 0, d).wait_send()
+    for i in range(half_chunks):
+        for s in range(pairs):
+            for d in range(n_narrow):
+                twin_copy(i, s - place, d).wait_send()
+    for s in range(pairs):
+        all_near(s - place, sent)
+    for j in range(1 - pairs, pairs):
+        for route in routes:
+            line_go(route, j, sent)
 
 
 def tail(n_wide, n_narrow, attended, picked, ffn_gain, final_gain, *weights):
@@ -394,7 +487,7 @@
     vmem = pl.BlockSpec(memory_space=pltpu.VMEM)
     hbm = pl.BlockSpec(memory_space=pl.ANY)
     near = n_narrow - 1
-    slots = 3 + 1 + near + pairs - 1
+    slots = 2 + 1 + 2 * near + pairs - 1
     dma = pltpu.SemaphoreType.DMA
     return pl.pallas_call(
         functools.partial(tail_kernel, n_wide, n_narrow),
@@ -417,6 +510,9 @@
             pltpu.VMEM((rows, w_gate.shape[1]), F32),
             pltpu.VMEM((mine, width // 2), BF16),
             pltpu.VMEM((mine, width // 2), BF16),
+            pltpu.VMEM((rows, LANES), F32),
+            pltpu.VMEM((mine, LANES), F32),
+            pltpu.VMEM((mine, LANES), F32),
             pltpu.VMEM((total_rows, width), BF16),
             pltpu.VMEM((total_rows, 128), F32),
             pltpu.VMEM((total_rows, 128), F32),
@@ -428,13 +524,16 @@
             dma((CHUNKS, near)),
             dma((CHUNKS, near)),
             dma((CHUNKS, near)),
-            dma((2,)),
-            dma((pairs,)),
-            dma((pairs,)),
-            dma((pairs, n_narrow)),
-            dma((pairs, n_narrow)),
-            dma((pairs, n_narrow)),
-            dma((pairs, n_narrow)),
+            dma((CHUNKS // 2 + 1,)),
+            dma((CHUNKS // 2 + 1,)),
+            dma((near,)),
+            dma((near,)),
+            dma((2 * n_narrow, pairs, 2)),
+            dma((2 * n_narrow, pairs, 2)),
+            dma((2, pairs, n_narrow)),
+            dma((2, pairs, n_narrow)),
+            dma((2, pairs, n_narrow)),
+            dma((2, pairs, n_narrow)),
             dma((slots,)),
             dma((slots,)),
         ],

time: 130 us -> 124 us (0.954)
  Pallas kernels: 114 us -> 107 us
    pallas_call x1, Pallas kernels: 96.3 us -> 89.9 us  [tail(): pl.pallas_call(functools.partial(tail_kernel, n_wide, n_narrow), out_shap...]
where the time goes in v2:
time: 124 us
  Pallas kernels  107 us (86%)
  matrix products  5.91 us (5%)
  local copies, waits for them, and re-layouts  5.17 us (4%)
  other arithmetic  4.57 us (4%)
    pallas_call x1, Pallas kernels, tail(): pl.pallas_call(functools.partial(tail_kernel, n_wide, n_narrow), out_shap...  89.9 us
    pallas_call x1, Pallas kernels, gather_rows(): pl.pallas_call(functools.partial(gather_kernel, n_narrow), out_shape=(sha...  17.5 us
    dot_general x2, matrix products, dot(): return jnp.dot(a, b, preferred_element_type=F32)  3.31 us
    sub x1, other arithmetic, on_device(): return (logits - stats[0][:, None], stats[1].reshape(-1, masked))  3.11 us

profile of v2, /device:TPU:0, one launch (start us, length us, event | category | flops | bytes accessed | tf_op | source)
XLA Modules:
  0.0 123.8 jit_solution(7349544164257016471)
XLA Ops:
  0.6 0.0 copy-start
  0.6 0.0 copy-start.2
  0.7 0.0 copy-start.1
  0.7 0.8 constant_dynamic-slice_fusion.1
  1.5 0.7 iota_compare_fusion.3
  2.3 0.0 copy-done
  2.3 0.0 copy-start.3
  2.3 1.1 constant_dynamic-slice_fusion.2
  3.3 0.1 copy.47
  3.4 0.0 copy-done.2
  3.5 0.0 copy-done.1
  3.5 17.5 %shard_map.149 = (bf16[128,4096]{1,0:T(8,128)(2,1)S(1)}, bf16[128,4096]{1,0:T(8,128)(2,1)S(1)}) custom-call(bf16[128,1024]{1,0:T(8,128)(2,1)S(1)} %bitcast.72, f32[1,4096]{1,0:T(1,128)S(1)} %bitcast.73), custom_call_target="tpu_custom_call" | custom-call | tf_op jit(solution)/shard_map/pallas_call | solution.py:76
  20.9 0.5 convolution_convert_fusion
  21.4 0.8 constant_dynamic-slice_fusion.picked
  22.2 2.0 %fusion.8 = bf16[128,256]{1,0:T(8,128)(2,1)S(1)} fusion(bf16[128,4096]{1,0:T(8,128)(2,1)S(1)} %get-tuple-element.6, bf16[4096,1024]{1,0:T(8,128)(2,1)} %param.19, s32[]{:T(128)S(6)} %select_n.34), kind=kOutput, calls=%fused_computation.17 | convolution fusion | flops 268468224 | bytes 3211268 | tf_op jit(solution)/shard_map/dot_general | solution.py:23
  24.2 0.0 copy-done.3
  24.2 1.3 %convolution_convert_fusion.2 = bf16[128,1024]{1,0:T(8,128)(2,1)S(1)} fusion(bf16[128,4096]{1,0:T(8,128)(2,1)S(1)} %get-tuple-element.6, bf16[4096,1024]{1,0:T(8,128)(2,1)S(1)} %copy-done.3), kind=kOutput, calls=%fused_computation.14 | convolution fusion | flops 1073872896 | bytes 9699328 | tf_op jit(solution)/shard_map/dot_general | solution.py:23
  25.5 0.3 fusion.6
  25.8 0.4 fusion.24
  26.2 0.5 bitcast_reduce_fusion
  26.7 0.1 fusion.12
  26.8 0.6 fusion.3
  27.4 0.3 fusion.16
  27.7 0.7 fusion.7
  28.4 0.2 copy.24
  28.6 0.8 copy.48
  29.3 89.9 %shard_map.150 = (f32[512,1024]{1,0:T(8,128)}, f32[2,512]{1,0:T(2,128)}) custom-call(bf16[128,1024]{1,0:T(8,128)(2,1)} %bitcast.77, bf16[32,4096]{1,0:T(8,128)(2,1)} %constant_dynamic-slice_fusion.picked, f32[1,4096]{1,0:T(1,128)} %bitcast.82, f32[1,4096]{1,0:T(1,128)} %bitcast.83, bf16[1024,4096]{1,0:T(8,128)(2,1)} %w_out.1, bf16[4096,256]{1,0:T(8,128)(2,1)} %w_gate.1, ...), custom_call_target="tpu_custom_call" | custom-call | tf_op jit(solution)/shard_map/pallas_call | solution.py:492
  119.2 0.8 slice_reduce_fusion
  120.0 3.1 %broadcast_subtract_fusion = f32[512,1024]{1,0:T(8,128)} fusion(f32[512,1024]{1,0:T(8,128)} %get-tuple-element.8, f32[512]{0:T(512)S(1)} %bitcast.84), kind=kLoop, calls=%fused_computation.18 | loop fusion | flops 524288 | bytes 4196352 | tf_op jit(solution)/shard_map/sub | solution.py:631
  123.1 0.7 reshape_squeeze.3
  (2 shorter events, 0.0 us)
Async XLA Ops:
  0.6 1.6 %copy-start = (bf16[2,512,4,256]{3,2,1,0:T(4,128)(2,1)S(1)}, bf16[2,512,4,256]{3,2,1,0:T(4,128)(2,1)}, u32[]{:S(2)}) copy-start(bf16[2,512,4,256]{3,2,1,0:T(4,128)(2,1)} %param.25) | copy-start | bytes 6291460
  0.6 2.8 %copy-start.2 = (f32[4096]{0:T(1024)S(1)}, f32[4096]{0:T(1024)}, u32[]{:S(2)}) copy-start(f32[4096]{0:T(1024)} %param.15) | copy-start | bytes 49156
  0.7 2.8 %copy-start.1 = (bf16[2,64,1024]{2,1,0:T(8,128)(2,1)S(1)}, bf16[2,64,1024]{2,1,0:T(8,128)(2,1)}, u32[]{:S(2)}) copy-start(bf16[2,64,1024]{2,1,0:T(8,128)(2,1)} %param.14) | copy-start | bytes 786436
  2.3 22.0 %copy-start.3 = (bf16[4096,1024]{1,0:T(8,128)(2,1)S(1)}, bf16[4096,1024]{1,0:T(8,128)(2,1)}, u32[]{:S(2)}) copy-start(bf16[4096,1024]{1,0:T(8,128)(2,1)} %param.18) | copy-start | bytes 25165828
